TPU v7x, 128 devices: a whole 4x4x4 slice. The times are simulated.
128 devices in a mesh: dp: 8 (over x, core), tensor: 16 (over z, y).
Axes of the slice: x: 4, y: 4, z: 4, core: 2. Of those that a mesh axis runs over, the one named last changes fastest.
Arguments:
- acts: bfloat16 [16384, 8192], P(('dp', 'tensor')), may hold values from -6 to 6
- cot_kv: bfloat16 [16384, 2048], P('dp', 'tensor'), may hold values from -0.09375 to 0.09375
- w_kv: bfloat16 [8192, 2048], P(None, 'tensor'), may hold values from -4 to 4
- feedback: bfloat16 [65536, 2048], P('dp', 'tensor'), may hold values from -3 to 3
- q_init: float32 [2048, 64], P('tensor'), may hold values from -6 to 6
Outputs:
- input_grad: bfloat16 [16384, 8192], P(('dp', 'tensor'))
- update: bfloat16 [8192, 2048], P(None, 'tensor')
- q_factor: float32 [2048, 64], P('tensor')
- new_feedback: bfloat16 [65536, 2048], P('dp', 'tensor')
All inputs are finite; a program needn't handle non-finite values.
Results may differ from a plain program's by a relative error of at most 0.019.
Values may be sent and summed in bfloat16 or wider, within the bound.
No kernel may reach another device: no remote copies, remote signals or barrier semaphores. Data moves between devices by JAX's collectives and lax.ppermute only.
A program may use at most 192 MiB of HBM per device.

v0:
```python
import jax
import jax.numpy as jnp
from jax import lax
from jax.sharding import PartitionSpec as P

HD = 128
RANK = 64


def gram_of(pmat):
    return jnp.einsum("mdr,mds->mrs", pmat, pmat, precision=lax.Precision.HIGHEST)


def apply_inverse(lower, pmat):
    return lax.linalg.triangular_solve(lower, pmat, left_side=False, lower=True, transpose_a=True)


def right_product(blocks, pmat):
    return jnp.einsum("dmh,mdr->mhr", blocks, pmat, precision=lax.Precision.HIGHEST)


def local(acts, cot_kv, w_kv, feedback, q_init):
    rows_dev, width = acts.shape
    ncol = cot_kv.shape[1]
    nmat = ncol // HD
    replicas = lax.axis_size("dp")
    part = cot_kv
    grad = lax.dot_general(
        lax.all_gather(acts, "tensor", axis=0, tiled=True),
        part,
        (((0,), (0,)), ((), ())),
        preferred_element_type=jnp.float32,
    )
    part = cot_kv
    input_grad = lax.psum_scatter(
        lax.dot_general(
            part, w_kv, (((1,), (1,)), ((), ())), preferred_element_type=jnp.float32
        ).astype(jnp.bfloat16),
        "tensor",
        scatter_dimension=0,
        tiled=True,
    )
    merged = feedback.astype(jnp.float32) + grad
    blocks = merged.reshape(width, nmat, HD)
    qmat = q_init.reshape(nmat, HD, RANK)
    local_p = jnp.einsum("dmh,mhr->mdr", blocks, qmat, precision=lax.Precision.HIGHEST)
    summed = lax.psum(local_p, "dp") / replicas
    lower = jnp.linalg.cholesky(gram_of(summed))
    phat = apply_inverse(lower, summed)
    q_local = right_product(blocks, phat)
    qfac = lax.psum(q_local, "dp") / replicas
    approx = jnp.einsum("mdr,mhr->dmh", phat, qfac, precision=lax.Precision.HIGHEST).reshape(
        width, ncol
    )
    new_feedback = (merged - approx).astype(jnp.bfloat16)
    return (input_grad, approx.astype(jnp.bfloat16), qfac.reshape(ncol, RANK), new_feedback)


def solution(mesh):
    placed = (
        P(("dp", "tensor"), None),
        P("dp", "tensor"),
        P(None, "tensor"),
        P("dp", "tensor"),
        P("tensor", None),
    )
    return jax.shard_map(
        local,
        mesh=mesh,
        in_specs=placed,
        out_specs=(
            P(("dp", "tensor"), None),
            P(None, "tensor"),
            P("tensor", None),
            P("dp", "tensor"),
        ),
        check_vma=False,
    )
```

profile of v0, /device:TPU:1, one launch (start us, length us, event | category | flops | bytes accessed | tf_op | source)
XLA Modules:
  0.0 505.8 jit_solution(2360252582829019889)
XLA Ops:
  7.2 0.0 copy-start
  7.2 0.0 copy-start.5
  7.2 0.0 all-gather.2.cloned.1.call-start
  7.2 0.7 all-gather.2.cloned.1.call-update
  7.9 0.0 copy-start.7
  7.9 0.0 all-reduce.2.cloned.1.call-start
  8.0 202.6 %all-gather.2.cloned.1.call-done = bf16[2048,8192]{1,0:T(8,128)(2,1)} async-done(((bf16[128,8192]{1,0:T(8,128)(2,1)}), bf16[2048,8192]{1,0:T(8,128)(2,1)}) %all-gather.2.cloned.1.call-update) | async-done | bytes 33554448 | tf_op jit(solution)/shard_map/all_gather | solution.py:29
  210.6 0.0 copy-done.5
  210.6 16.4 %convolution_add_fusion = f32[8192,128]{1,0:T(8,128)S(1)} fusion(bf16[2048,8192]{1,0:T(8,128)(2,1)} %all-gather.2.cloned.1.call-done, bf16[2048,128]{1,0:T(8,128)(2,1)S(1)} %copy-done.5, bf16[8192,128]{1,0:T(8,128)(2,1)} %param.8), kind=kOutput, calls=%fused_computation.2 | convolution fusion | flops 4297064448 | bytes 40370176 | tf_op jit(solution)/shard_map/dot_general | solution.py:28
  227.1 0.0 copy-start.2
  227.1 2.0 copy-done.2
  229.1 0.0 copy-done.7
  229.1 6.0 %convolution_bitcast_fusion.1 = f32[1,8192,64]{1,2,0:T(8,128)} fusion(f32[8192,128]{1,0:T(8,128)S(1)} %convolution_add_fusion, f32[128,64]{0,1:T(8,128)S(1)} %copy-done.7), kind=kOutput, calls=%fused_computation.3 | convolution fusion | flops 805306368 | bytes 6324224 | tf_op jit(solution)/shard_map/dmh,mhr->mdr/dot_general | solution.py:46
  235.1 0.0 all-reduce.2.cloned.1.call-update
  235.1 0.2 reduce-scatter.2.cloned.1.call-start
  235.4 0.0 copy-done
  235.4 14.5 %convolution_convert_fusion = bf16[2048,8192]{1,0:T(8,128)(2,1)} fusion(bf16[2048,128]{1,0:T(8,128)(2,1)S(1)} %copy-done.5, bf16[8192,128]{1,0:T(8,128)(2,1)S(1)} %copy-done), kind=kOutput, calls=%fused_computation | convolution fusion | flops 4311744512 | bytes 36175872 | tf_op jit(solution)/shard_map/dot_general | solution.py:36
  249.8 0.0 reduce-scatter.2.cloned.1.call-update
  249.9 48.7 %all-reduce.2.cloned.1.call-done = f32[1,8192,64]{1,2,0:T(8,128)} async-done(((f32[1,8192,64]{1,2,0:T(8,128)}), f32[1,8192,64]{1,2,0:T(8,128)}) %all-reduce.2.cloned.1.call-update) | async-done | bytes 2097168 | tf_op jit(solution)/shard_map/psum | solution.py:47
  298.6 4.1 fusion.2
  302.7 0.1 copy.10
  302.8 5.8 %custom-call.7 = f32[1,64,64]{2,1,0:T(8,128)S(1)} custom-call(f32[1,64,64]{2,1,0:T(8,128)S(1)} %fusion.9), custom_call_target="Cholesky" | custom-call | tf_op jit(solution)/shard_map/jit(cholesky)/cholesky | solution.py:48
  308.7 0.6 compare_reduce_fusion
  309.4 0.7 fusion.8
  310.0 4.9 custom-call.8
  314.9 0.0 copy-start.3
  314.9 3.8 fusion
  318.7 0.0 copy-done.3
  318.8 0.0 copy-start.4
  318.8 2.9 convolution_bitcast_fusion.2
  321.7 0.0 copy-done.4
  321.7 25.0 %psum.15 = f32[1,128,64]{1,2,0:T(8,128)S(1)} all-reduce(f32[1,128,64]{1,2,0:T(8,128)S(1)} %convolution_bitcast_fusion.2), channel_id=1, replica_groups=mesh['dp'=8,'tensor'=16] {'dp'}, use_global_device_ids=true, to_apply=%region_4.5 | all-reduce | flops 8192 | bytes 65536 | tf_op jit(solution)/shard_map/psum | solution.py:51
  346.7 0.0 copy-start.6
  346.7 0.0 copy-start.1
  346.7 10.5 %subtract_convert_fusion = (bf16[8192,128]{1,0:T(8,128)(2,1)}, bf16[8192,128]{1,0:T(8,128)(2,1)}) fusion(f32[8192,128]{1,0:T(8,128)} %copy-done.2, f32[128,64]{0,1:T(8,128)S(1)} %multiply_bitcast_fusion, f32[8192,64]{0,1:T(8,128)} %copy-done.4), kind=kOutput, calls=%fused_computation.4 | convolution fusion | flops 808452096 | bytes 10518528 | tf_op jit(solution)/shard_map/mdr,mhr->dmh/dot_general | solution.py:52
  357.3 0.0 copy-done.6
  357.3 142.0 %reduce-scatter.2.cloned.1.call-done = bf16[128,8192]{1,0:T(8,128)(2,1)} async-done(((bf16[2048,8192]{1,0:T(8,128)(2,1)}), bf16[128,8192]{1,0:T(8,128)(2,1)}) %reduce-scatter.2.cloned.1.call-update) | async-done | bytes 2097168 | tf_op jit(solution)/shard_map/reduce_scatter | solution.py:35
  499.3 0.0 copy-done.1
  (3 shorter events, 0.0 us)
Async XLA Ops:
  7.2 228.2 %copy-start = (bf16[8192,128]{1,0:T(8,128)(2,1)S(1)}, bf16[8192,128]{1,0:T(8,128)(2,1)}, u32[]{:S(2)}) copy-start(bf16[8192,128]{1,0:T(8,128)(2,1)} %param.7) | copy-start | bytes 6291460
  7.2 203.4 %copy-start.5 = (bf16[2048,128]{1,0:T(8,128)(2,1)S(1)}, bf16[2048,128]{1,0:T(8,128)(2,1)}, u32[]{:S(2)}) copy-start(bf16[2048,128]{1,0:T(8,128)(2,1)} %param.6) | copy-start | bytes 1572868
  7.2 203.4 %all-gather.2.cloned.1.call-start = ((), (), s32[]{:S(2)}) async-start(), calls=%async_computation.2 | async-start | bytes 35651584 | tf_op jit(solution)/shard_map/all_gather | solution.py:29
  7.9 221.2 %copy-start.7 = (f32[128,64]{0,1:T(8,128)S(1)}, f32[128,64]{0,1:T(8,128)}, u32[]{:S(2)}) copy-start(f32[128,64]{0,1:T(8,128)} %param.9) | copy-start | bytes 98308
  7.9 290.6 %all-reduce.2.cloned.1.call-start = ((), (), s32[]{:S(2)}) async-start(), calls=%async_computation.3 | async-start | bytes 4194304 | tf_op jit(solution)/shard_map/psum | solution.py:47
  227.1 2.0 copy-start.2
  235.1 264.2 %reduce-scatter.2.cloned.1.call-start = ((), (), s32[]{:S(2)}) async-start(), calls=%async_computation.1 | async-start | bytes 35651584 | tf_op jit(solution)/shard_map/reduce_scatter | solution.py:35
  314.9 3.8 copy-start.3
  318.8 2.9 copy-start.4
  346.7 10.6 %copy-start.6 = (f32[128,64]{0,1:T(8,128)}, f32[128,64]{0,1:T(8,128)S(1)}, u32[]{:S(2)}) copy-start(f32[128,64]{0,1:T(8,128)S(1)} %multiply_bitcast_fusion) | copy-start | bytes 98308
  346.7 152.6 %copy-start.1 = (bf16[8192,128]{1,0:T(8,128)(2,1)S(1)}, bf16[8192,128]{1,0:T(8,128)(2,1)}, u32[]{:S(2)}) copy-start(bf16[8192,128]{1,0:T(8,128)(2,1)} %param.7) | copy-start | bytes 6291460
Sparse Core Ops, SparseCore 0:
  10.2 200.4 all-gather.1
  235.3 63.2 all-reduce.1
  302.7 196.5 reduce-scatter.1
where the time goes:
time: 506 us
  waiting for transfers between devices  394 us (78%)
  matrix products  58.3 us (12%)
  blocking collectives  25 us (5%)
  between operations  13.9 us (3%)
  other arithmetic  12.1 us (2%)
    all_gather x1, waiting for transfers between devices, local(): lax.all_gather(acts, 'tensor', axis=0, tiled=True)  203 us
    reduce_scatter x1, waiting for transfers between devices, local(): lax.psum_scatter(lax.dot_general(part, w_kv, (((1,), (1,)), ((), ())), pr...  142 us
    psum x1, waiting for transfers between devices, local(): summed = lax.psum(local_p, 'dp') / replicas  48.7 us
    psum x1, blocking collectives, local(): qfac = lax.psum(q_local, 'dp') / replicas  25 us
    dot_general x1, matrix products, local(): lax.dot_general(lax.all_gather(acts, 'tensor', axis=0, tiled=True), part,...  16.4 us
    dot_general x1, matrix products, local(): lax.dot_general(part, w_kv, (((1,), (1,)), ((), ())), preferred_element_t...  14.5 us
    dot_general x1, matrix products, local(): jnp.einsum('mdr,mhr->dmh', phat, qfac, precision=lax.Precision.HIGHEST)  10.5 us
  transfers between devices with their start and end apart: 3, of which 3 were waited for; matrix products, arithmetic and copies ran while one was open for 9% of the time, Pallas kernels for 0%

commit v1 on v0

v1 whole, which is shorter than its diff:
```python
import functools

import jax
import jax.numpy as jnp
from jax import lax
from jax.experimental import pallas as pl
from jax.experimental.pallas import tpu as pltpu
from jax.sharding import PartitionSpec as P

HD = 128
RANK = 64
SIDE = 4
TILE = 512
F32 = jnp.float32
BF16 = jnp.bfloat16
HI = lax.Precision.HIGHEST


def along_tensor(array, dz, dy):
    perm = [
        (z * SIDE + y, (z + dz) % SIDE * SIDE + (y + dy) % SIDE)
        for z in range(SIDE)
        for y in range(SIDE)
    ]
    return lax.ppermute(array, "tensor", perm)


def along_dp(array, dx, dc):
    perm = [
        (x * 2 + c, (x + dx) % SIDE * 2 + (c + dc) % 2)
        for x in range(SIDE)
        for c in range(2)
    ]
    return lax.ppermute(array, "dp", perm)


def cost(flops, moved):
    return pl.CostEstimate(flops=int(flops), bytes_accessed=int(moved), transcendentals=0)


def rows_spec(rows, cols):
    return pl.BlockSpec((rows, cols), lambda j: (j, 0))


def cols_spec(rows, cols):
    return pl.BlockSpec((rows, cols), lambda j: (0, j))


def whole_spec(rows, cols):
    return pl.BlockSpec((rows, cols), lambda j: (0, 0))


def grad_kernel(a0, a1, a2lo, a2hi, a3, cmat, own, b1, b2lo, b2hi, b3):
    j = pl.program_id(0)
    mid = pl.num_programs(0) // 2
    tokens = jnp.concatenate([a0[...], a1[...], a2lo[...], a2hi[...], a3[...]], axis=0)
    part = lax.dot_general(
        tokens, cmat[...], (((0,), (0,)), ((), ())), preferred_element_type=F32
    )
    own[...] = part[:, :HD]
    b1[...] = part[:, HD : 2 * HD].astype(BF16)
    b3[...] = part[:, 3 * HD :].astype(BF16)
    across = part[:, 2 * HD : 3 * HD].astype(BF16)

    @pl.when(j < mid)
    def _():
        b2lo[...] = across

    @pl.when(j >= mid)
    def _():
        b2hi[...] = across


def grad_parts(a0, a1, a2lo, a2hi, a3, cmat):
    rows, width = a0.shape
    steps = width // TILE
    mid = steps // 2
    return pl.pallas_call(
        grad_kernel,
        grid=(steps,),
        in_specs=[
            cols_spec(rows, TILE),
            cols_spec(rows, TILE),
            cols_spec(rows // 2, TILE),
            cols_spec(rows // 2, TILE),
            cols_spec(rows, TILE),
            whole_spec(SIDE * rows, SIDE * HD),
        ],
        out_specs=[
            rows_spec(TILE, HD),
            rows_spec(TILE, HD),
            pl.BlockSpec((TILE, HD), lambda j: (jnp.minimum(j, mid - 1), 0)),
            pl.BlockSpec((TILE, HD), lambda j: (jnp.maximum(j - mid, 0), 0)),
            rows_spec(TILE, HD),
        ],
        out_shape=[
            jax.ShapeDtypeStruct((width, HD), F32),
            jax.ShapeDtypeStruct((width, HD), BF16),
            jax.ShapeDtypeStruct((width // 2, HD), BF16),
            jax.ShapeDtypeStruct((width // 2, HD), BF16),
            jax.ShapeDtypeStruct((width, HD), BF16),
        ],
        cost_estimate=cost(2 * width * SIDE * SIDE * rows * HD, 9 * width * HD * 2),
        name="grad_parts",
    )(a0, a1, a2lo, a2hi, a3, cmat)


def input_kernel(w0, wg, cmat, own, b1, b2lo, b2hi, b3):
    rows = own.shape[0]
    weights = jnp.concatenate([w0[...], wg[0, 0], wg[0, 1], wg[0, 2]], axis=1)
    part = lax.dot_general(
        cmat[...], weights, (((1,), (1,)), ((), ())), preferred_element_type=F32
    )
    own[...] = part[:rows]
    b1[...] = part[rows : 2 * rows].astype(BF16)
    b2lo[...] = part[2 * rows : 2 * rows + rows // 2].astype(BF16)
    b2hi[...] = part[2 * rows + rows // 2 : 3 * rows].astype(BF16)
    b3[...] = part[3 * rows :].astype(BF16)


def input_parts(weights, gathered, cmat, part):
    width = weights.shape[0] // 2
    rows = cmat.shape[0] // SIDE
    pieces, kinds, tile, _ = gathered.shape
    first = part * pieces
    return pl.pallas_call(
        input_kernel,
        grid=(pieces,),
        in_specs=[
            pl.BlockSpec((tile, HD), lambda j: (first + j, 0)),
            pl.BlockSpec((1, kinds // 2, tile, HD), lambda j: (j, part, 0, 0)),
            whole_spec(SIDE * rows, SIDE * HD),
        ],
        out_specs=[
            cols_spec(rows, tile),
            cols_spec(rows, tile),
            cols_spec(rows // 2, tile),
            cols_spec(rows // 2, tile),
            cols_spec(rows, tile),
        ],
        out_shape=[
            jax.ShapeDtypeStruct((rows, width), F32),
            jax.ShapeDtypeStruct((rows, width), BF16),
            jax.ShapeDtypeStruct((rows // 2, width), BF16),
            jax.ShapeDtypeStruct((rows // 2, width), BF16),
            jax.ShapeDtypeStruct((rows, width), BF16),
        ],
        cost_estimate=cost(2 * width * SIDE * SIDE * rows * HD, 9 * width * HD * 2),
        name="input_parts",
    )(weights, gathered, cmat)


def merge_kernel(fb, own, left, right, qrows, merged, keep, give):
    total = fb[...].astype(F32) + own[...] + (left[...].astype(F32) + right[...].astype(F32))
    merged[...] = total
    share = lax.dot_general(
        qrows[...], total, (((1,), (1,)), ((), ())), precision=HI, preferred_element_type=F32
    )
    keep[...] = share[: RANK // 2]
    give[...] = share[RANK // 2 :]


def merge(feedback, own, left, right, qrows, part):
    width = own.shape[0]
    tile = 1024
    steps = width // tile
    return pl.pallas_call(
        merge_kernel,
        grid=(steps,),
        in_specs=[
            pl.BlockSpec((tile, HD), lambda j: (part * steps + j, 0)),
            rows_spec(tile, HD),
            rows_spec(tile, HD),
            rows_spec(tile, HD),
            whole_spec(RANK, HD),
        ],
        out_specs=[
            rows_spec(tile, HD),
            cols_spec(RANK // 2, tile),
            cols_spec(RANK // 2, tile),
        ],
        out_shape=[
            jax.ShapeDtypeStruct((width, HD), F32),
            jax.ShapeDtypeStruct((RANK // 2, width), F32),
            jax.ShapeDtypeStruct((RANK // 2, width), F32),
        ],
        cost_estimate=cost(12 * width * RANK * HD, 14 * width * HD),
        name="merge",
    )(feedback, own, left, right, qrows)


def gram_kernel(pt, merged, gram, right):
    @pl.when(pl.program_id(0) == 0)
    def _():
        gram[...] = jnp.zeros_like(gram)
        right[...] = jnp.zeros_like(right)

    left = pt[...]
    gram[...] += lax.dot_general(
        left, left, (((1,), (1,)), ((), ())), precision=HI, preferred_element_type=F32
    )
    right[...] += jnp.dot(left, merged[...], precision=HI, preferred_element_type=F32)


def gram_of(pt, merged):
    width = merged.shape[0]
    tile = 1024
    return pl.pallas_call(
        gram_kernel,
        grid=(width // tile,),
        in_specs=[cols_spec(RANK, tile), rows_spec(tile, HD)],
        out_specs=[whole_spec(RANK, RANK), whole_spec(RANK, HD)],
        out_shape=[
            jax.ShapeDtypeStruct((RANK, RANK), F32),
            jax.ShapeDtypeStruct((RANK, HD), F32),
        ],
        cost_estimate=cost(12 * width * RANK * (RANK + HD), 6 * width * HD),
        name="gram",
    )(pt, merged)


def inverse_kernel(gram_a, gram_b, out):
    row = lax.broadcasted_iota(jnp.int32, (RANK, RANK), 0)
    col = lax.broadcasted_iota(jnp.int32, (RANK, RANK), 1)
    eye = jnp.where(row == col, 1.0, 0.0).astype(F32)
    mat = jnp.concatenate([gram_a[...] + gram_b[...], eye], axis=1)
    below = lax.broadcasted_iota(jnp.int32, (RANK, 1), 0)
    for k in range(RANK - 1):
        pivot = mat[k : k + 1, :]
        column = mat[:, k : k + 1]
        factor = jnp.where(below > k, column / mat[k : k + 1, k : k + 1], 0.0)
        mat = mat - factor * pivot
    diag = jnp.sum(jnp.where(row == col, mat[:, :RANK], 0.0), axis=1, keepdims=True)
    out[...] = mat[:, RANK:] / jnp.sqrt(diag)


def inverse_factor(gram_a, gram_b):
    return pl.pallas_call(
        inverse_kernel,
        out_shape=jax.ShapeDtypeStruct((RANK, RANK), F32),
        cost_estimate=cost(RANK * RANK * RANK * 400, RANK * RANK * 16),
        name="inverse_factor",
    )(gram_a, gram_b)


def final_kernel(inv, rsum, pt_a, pt_b, mg_a, mg_b, qt, update, newfb, zmat):
    j = pl.program_id(0)
    mid = pl.num_programs(0) // 2

    @pl.when(j == 0)
    def _():
        right = jnp.dot(inv[...], rsum[...], precision=HI, preferred_element_type=F32) * 0.125
        qt[...] = right
        zmat[...] = lax.dot_general(
            inv[...], right, (((0,), (0,)), ((), ())), precision=HI, preferred_element_type=F32
        )

    def finish(pt, mg):
        approx = lax.dot_general(
            pt[...], zmat[...], (((0,), (0,)), ((), ())), precision=HI, preferred_element_type=F32
        )
        update[...] = approx.astype(BF16)
        newfb[...] = (mg[...] - approx).astype(BF16)

    @pl.when(j < mid)
    def _():
        finish(pt_a, mg_a)

    @pl.when(j >= mid)
    def _():
        finish(pt_b, mg_b)


def final(inv, rsum, pts, mgs):
    half = mgs[0].shape[0]
    tile = 1024
    mid = half // tile
    lo = lambda j: jnp.minimum(j, mid - 1)
    hi = lambda j: jnp.maximum(j - mid, 0)
    return pl.pallas_call(
        final_kernel,
        grid=(2 * mid,),
        in_specs=[
            whole_spec(RANK, RANK),
            whole_spec(RANK, HD),
            pl.BlockSpec((RANK, tile), lambda j: (0, lo(j))),
            pl.BlockSpec((RANK, tile), lambda j: (0, hi(j))),
            pl.BlockSpec((tile, HD), lambda j: (lo(j), 0)),
            pl.BlockSpec((tile, HD), lambda j: (hi(j), 0)),
        ],
        out_specs=[
            whole_spec(RANK, HD),
            rows_spec(tile, HD),
            rows_spec(tile, HD),
        ],
        out_shape=[
            jax.ShapeDtypeStruct((RANK, HD), F32),
            jax.ShapeDtypeStruct((2 * half, HD), BF16),
            jax.ShapeDtypeStruct((2 * half, HD), BF16),
        ],
        scratch_shapes=[pltpu.VMEM((RANK, HD), F32)],
        cost_estimate=cost(24 * half * RANK * HD, 24 * half * HD),
        name="final",
    )(inv, rsum, *pts, *mgs)


def gather_line(block, step):
    rows = block.shape[0]
    before = step(block, 1)
    after = step(block, -1)
    across_lo = step(before[: rows // 2], 1)
    across_hi = step(after[rows // 2 :], -1)
    return block, after, across_lo, across_hi, before


def scatter_line(b1, b2lo, b2hi, b3, step):
    rows = b1.shape[0]
    low = step(b2lo, 1)
    high = step(b2hi, -1)
    up = jnp.concatenate(
        [(b1[: rows // 2].astype(F32) + low.astype(F32)).astype(BF16), b1[rows // 2 :]], axis=0
    )
    down = jnp.concatenate(
        [b3[: rows // 2], (b3[rows // 2 :].astype(F32) + high.astype(F32)).astype(BF16)], axis=0
    )
    return step(up, 1), step(down, -1)


def sum_chips(array):
    ahead = along_dp(array, 1, 0).astype(F32)
    behind = along_dp(array, -1, 0).astype(F32)
    across = along_dp(array, 2, 0).astype(F32)
    return (array.astype(F32) + across) + (ahead + behind)


def sum_left(keep, give, core):
    chip = (keep + along_dp(give, 0, 1)).astype(BF16)
    mine = sum_chips(chip)
    theirs = along_dp(mine, 0, 1)
    first = jnp.where(core == 0, mine, theirs)
    second = jnp.where(core == 0, theirs, mine)
    return jnp.concatenate([first, second], axis=0)


def sum_right(part):
    return sum_chips(part + along_dp(part, 0, 1))


def local(acts, cot_kv, w_kv, feedback, q_init):
    tokens, width = acts.shape
    half = width // 2
    replicas = lax.axis_size("dp")
    place = lax.axis_index("dp")
    core = place % 2
    spot = lax.axis_index("tensor")
    z, y = spot // SIDE, spot % SIDE
    in_y = lambda array, k: along_tensor(array, 0, k)
    in_z = lambda array, k: along_tensor(array, k, 0)

    parts = (
        gather_line(acts[:, :half], in_y),
        gather_line(acts[:, half:], in_z),
    )

    blocks = cot_kv.reshape(SIDE, SIDE, tokens, HD)
    blocks = jnp.concatenate([blocks, blocks], axis=1)
    blocks = jnp.concatenate([blocks, blocks], axis=0)
    blocks = lax.dynamic_slice(blocks, (z, y, 0, 0), (SIDE, SIDE, tokens, HD))
    piece = half // replicas
    w_lo = lax.dynamic_slice(w_kv, (place * piece, 0), (piece, HD))
    w_hi = lax.dynamic_slice(w_kv, (half + place * piece, 0), (piece, HD))
    flat = SIDE * tokens
    cols = {0: blocks[0].reshape(flat, HD)}
    rows = {0: blocks[:, 0].reshape(flat, HD)}
    w_parts = {}
    for k in range(1, SIDE):
        got = in_z(jnp.concatenate([blocks[k].reshape(flat, HD), w_lo], axis=0), k)
        cols[SIDE - k], w_parts[SIDE - k - 1] = got[:flat], got[flat:]
        got = in_y(jnp.concatenate([blocks[:, k].reshape(flat, HD), w_hi], axis=0), k)
        rows[SIDE - k], w_parts[2 * SIDE - k - 2] = got[:flat], got[flat:]
    cmat = (
        jnp.concatenate([cols[k] for k in range(SIDE)], axis=1),
        jnp.concatenate([rows[k] for k in range(SIDE)], axis=1),
    )
    gathered = lax.all_gather(
        jnp.stack([w_parts[k] for k in range(2 * SIDE - 2)]), "dp", axis=0
    )

    qcols = q_init.T
    qrows = jnp.where(
        core == 0, qcols, jnp.concatenate([qcols[RANK // 2 :], qcols[: RANK // 2]], axis=0)
    )

    mgs, pts, grams, rights = [], [], [], []
    for part, step in ((0, in_z), (1, in_y)):
        own, b1, b2lo, b2hi, b3 = grad_parts(*parts[part], cmat[part])
        left, right = scatter_line(b1, b2lo, b2hi, b3, step)
        merged, keep, give = merge(feedback, own, left, right, qrows, part)
        pt = sum_left(keep, give, core)
        gram, share = gram_of(pt, merged)
        mgs.append(merged)
        pts.append(pt)
        grams.append(gram)
        rights.append(share)

    ig = []
    for part, step in ((0, in_y), (1, in_z)):
        own, b1, b2lo, b2hi, b3 = input_parts(w_kv, gathered, cmat[part], part)
        left, right = scatter_line(b1, b2lo, b2hi, b3, step)
        ig.append((own + (left.astype(F32) + right.astype(F32))).astype(BF16))
    input_grad = jnp.concatenate(ig, axis=1)

    inv = inverse_factor(*grams)
    rsum = sum_right(rights[0] + rights[1])
    qt, update, new_feedback = final(inv, rsum, pts, mgs)
    return input_grad, update, qt.T, new_feedback


def solution(mesh):
    placed = (
        P(("dp", "tensor"), None),
        P("dp", "tensor"),
        P(None, "tensor"),
        P("dp", "tensor"),
        P("tensor", None),
    )
    return jax.shard_map(
        local,
        mesh=mesh,
        in_specs=placed,
        out_specs=(
            P(("dp", "tensor"), None),
            P(None, "tensor"),
            P("tensor", None),
            P("dp", "tensor"),
        ),
        check_vma=False,
    )
```

time: 506 us -> 279 us (0.55)
  waiting for transfers between devices: 394 us -> 85.6 us
  Pallas kernels: 0 us -> 71.7 us
  starting transfers between devices: 0.3 us -> 64.9 us
  matrix products: 58.3 us -> 0 us
  blocking collectives: 25 us -> 0 us
  local copies, waits for them, and re-layouts: 2.16 us -> 14.8 us
  other arithmetic: 12.1 us -> 23.9 us
    all_gather x1, waiting for transfers between devices: 203 us -> 0.01 us  [local(): lax.all_gather(jnp.stack([w_parts[k] for k in range(2 * SIDE - 2)]), 'dp'...]
    reduce_scatter x1 -> x0, waiting for transfers between devices: 142 us -> none  [local(): lax.psum_scatter(lax.dot_general(part, w_kv, (((1,), (1,)), ((), ())), pr...]
    ppermute x0 -> x44, waiting for transfers between devices: none -> 85.6 us  [the longest x30 64.6 us: along_tensor(): return lax.ppermute(array, 'tensor', perm)]
    pallas_call x0 -> x10, Pallas kernels: none -> 71.7 us  [the longest x2 17.6 us: grad_parts(): pl.pallas_call(grad_kernel, grid=(steps,), in_specs=[cols_spec(rows, TILE...]
    ppermute x0 -> x44, starting transfers between devices: none -> 64.9 us  [the longest x30 45.5 us: along_tensor(): return lax.ppermute(array, 'tensor', perm)]
    dot_general x6 -> x0, matrix products: 54.5 us -> none  [the longest x1 16.4 us: local(): lax.dot_general(lax.all_gather(acts, 'tensor', axis=0, tiled=True), part,...]
    psum x1 -> x0, waiting for transfers between devices: 48.7 us -> none  [local(): summed = lax.psum(local_p, 'dp') / replicas]
    psum x1 -> x0, blocking collectives: 25 us -> none  [local(): qfac = lax.psum(q_local, 'dp') / replicas]
  transfers between devices with their start and end apart: 3 -> 45, of which waited for: 3 -> 18; matrix products, arithmetic and copies ran while one was open for 9% -> 11% of each run, Pallas kernels for 0% -> 23%
where the time goes in v1:
time: 279 us; the launch traced here: 275 us
  waiting for transfers between devices  85.6 us (31%)
  Pallas kernels  71.7 us (26%)
  starting transfers between devices  64.9 us (23%)
  other arithmetic  23.9 us (9%)
  local copies, waits for them, and re-layouts  14.8 us (5%)
  between operations  14.5 us (5%)
    ppermute x30, waiting for transfers between devices, along_tensor(): return lax.ppermute(array, 'tensor', perm)  64.6 us
    ppermute x30, starting transfers between devices, along_tensor(): return lax.ppermute(array, 'tensor', perm)  45.5 us
    ppermute x14, waiting for transfers between devices, along_dp(): return lax.ppermute(array, 'dp', perm)  21 us
    ppermute x14, starting transfers between devices, along_dp(): return lax.ppermute(array, 'dp', perm)  19.4 us
    pallas_call x2, Pallas kernels, grad_parts(): pl.pallas_call(grad_kernel, grid=(steps,), in_specs=[cols_spec(rows, TILE...  17.6 us
    pallas_call x2, Pallas kernels, input_parts(): pl.pallas_call(input_kernel, grid=(pieces,), in_specs=[pl.BlockSpec((tile...  16.5 us
    pallas_call x2, Pallas kernels, merge(): pl.pallas_call(merge_kernel, grid=(steps,), in_specs=[pl.BlockSpec((tile,...  11.5 us
    pallas_call x1, Pallas kernels, final(): pl.pallas_call(final_kernel, grid=(2 * mid,), in_specs=[whole_spec(RANK,...  9.91 us
  transfers between devices with their start and end apart: 45, of which 18 were waited for; matrix products, arithmetic and copies ran while one was open for 11% of the time, Pallas kernels for 23%

profile of v1, /device:TPU:1, one launch (start us, length us, event | category | flops | bytes accessed | tf_op | source)
XLA Modules:
  0.0 275.4 jit_solution(11107287744094712612)
XLA Ops:
  7.2 2.7 fusion.9
  10.0 4.6 %collective-permute-start.27 = (bf16[128,4096]{1,0:T(8,128)(2,1)}, bf16[128,4096]{1,0:T(8,128)(2,1)}, u32[]{:S(2)}, u32[]{:S(2)}) collective-permute-start(bf16[128,4096]{1,0:T(8,128)(2,1)} %get-tuple-element.70.a0), channel_id=1, source_target_pairs={{0,12},{1,13},{2,14},{3,15},{4,0},{5,1},{6,2},{7,3},{8,4},{9,5},{1... | collective-permute-start | bytes 3145736 | tf_op jit(solution)/shard_map/ppermute | solution.py:25
  16.1 2.7 collective-permute-start
  18.9 3.0 %collective-permute-start.4 = (bf16[1024,128]{1,0:T(8,128)(2,1)S(1)}, bf16[1024,128]{1,0:T(8,128)(2,1)S(1)}, u32[]{:S(2)}, u32[]{:S(2)}) collective-permute-start(bf16[1024,128]{1,0:T(8,128)(2,1)S(1)} %get-tuple-element.87), channel_id=1, source_target_pairs={{0,2},{1,3},{2,0},{3,1},{4,6},{5,7},{6,4},{7,5},{8,10},{9,11},{10,... | collective-permute-start | bytes 786440 | tf_op jit(solution)/shard_map/ppermute | solution.py:25
  22.3 19.9 %collective-permute-done = bf16[1024,128]{1,0:T(8,128)(2,1)S(1)} collective-permute-done((bf16[1024,128]{1,0:T(8,128)(2,1)S(1)}, bf16[1024,128]{1,0:T(8,128)(2,1)S(1)}, u32[]{:S(2)}, u32[]{:S(2)}) %collective-permute-start) | collective-permute-done | bytes 262176 | tf_op jit(solution)/shard_map/ppermute | solution.py:25
  42.2 2.7 collective-permute-start.3
  44.9 2.0 collective-permute-start.1
  47.0 1.9 collective-permute-start.2
  49.8 2.7 collective-permute-done.1
  52.9 6.9 %collective-permute-done.2 = bf16[1024,128]{1,0:T(8,128)(2,1)S(1)} collective-permute-done((bf16[1024,128]{1,0:T(8,128)(2,1)S(1)}, bf16[1024,128]{1,0:T(8,128)(2,1)S(1)}, u32[]{:S(2)}, u32[]{:S(2)}) %collective-permute-start.2) | collective-permute-done | bytes 262176 | tf_op jit(solution)/shard_map/ppermute | solution.py:25
  62.1 2.7 collective-permute-start.30
  65.7 7.7 %collective-permute-done.15.a3 = bf16[128,4096]{1,0:T(8,128)(2,1)S(1)} collective-permute-done((bf16[128,4096]{1,0:T(8,128)(2,1)S(1)}, bf16[128,4096]{1,0:T(8,128)(2,1)S(1)}, u32[]{:S(2)}, u32[]{:S(2)}) %collective-permute-start.15) | collective-permute-done | bytes 1048608 | tf_op jit(solution)/shard_map/ppermute | solution.py:25
  75.2 2.7 collective-permute-start.17
  78.7 8.8 %grad_parts.3 = (f32[4096,128]{1,0:T(8,128)}, bf16[4096,128]{1,0:T(8,128)(2,1)}, bf16[2048,128]{1,0:T(8,128)(2,1)}, bf16[2048,128]{1,0:T(8,128)(2,1)}, bf16[4096,128]{1,0:T(8,128)(2,1)}) custom-call(bf16[128,4096]{1,0:T(8,128)(2,1)} %get-tuple-element.70.a0, bf16[128,4096]{1,0:T(8,128)(2,1)} %collective-permute-done.27.a1, bf16[64,4096]{1,0:T(8,128)(2,1)} %copy-done.21, ...), custom_call_target="tpu_custom_call" | custom-call | flops 2147483648 | bytes 9437184 | tf_op jit(solution)/shard_map/grad_parts/pallas_call | solution.py:78
  90.0 2.7 collective-permute-start.33
  92.8 8.8 %grad_parts.2 = (f32[4096,128]{1,0:T(8,128)}, bf16[4096,128]{1,0:T(8,128)(2,1)}, bf16[2048,128]{1,0:T(8,128)(2,1)}, bf16[2048,128]{1,0:T(8,128)(2,1)}, bf16[4096,128]{1,0:T(8,128)(2,1)}) custom-call(bf16[128,4096]{1,0:T(8,128)(2,1)} %copy-done.12, bf16[128,4096]{1,0:T(8,128)(2,1)} %copy-done.17, bf16[64,4096]{1,0:T(8,128)(2,1)} %collective-permute-done.16.a2lo, ...), custom_call_target="tpu_custom_call" | custom-call | flops 2147483648 | bytes 9437184 | tf_op jit(solution)/shard_map/grad_parts/pallas_call | solution.py:78
  103.7 2.8 %collective-permute-start.20 = (bf16[2048,128]{1,0:T(8,128)(2,1)}, bf16[2048,128]{1,0:T(8,128)(2,1)S(1)}, u32[]{:S(2)}, u32[]{:S(2)}) collective-permute-start(bf16[2048,128]{1,0:T(8,128)(2,1)} %get-tuple-element.51), channel_id=1, source_target_pairs={{0,12},{1,13},{2,14},{3,15},{4,0},{5,1},{6,2},{7,3},{8,4},{9,5},{1... | collective-permute-start | bytes 1572872 | tf_op jit(solution)/shard_map/ppermute | solution.py:25
  110.2 2.7 collective-permute-start.34
  112.8 2.0 collective-permute-done.18
  116.3 2.6 collective-permute-start.21
  119.6 10.8 %collective-permute-done.32.left = bf16[4096,128]{1,0:T(8,128)(2,1)} collective-permute-done((bf16[4096,128]{1,0:T(8,128)(2,1)}, bf16[4096,128]{1,0:T(8,128)(2,1)}, u32[]{:S(2)}, u32[]{:S(2)}) %collective-permute-start.32) | collective-permute-done | bytes 1048608 | tf_op jit(solution)/shard_map/ppermute | solution.py:25
  130.4 5.7 %merge.3 = (f32[4096,128]{1,0:T(8,128)}, f32[32,4096]{1,0:T(8,128)}, f32[32,4096]{1,0:T(8,128)}) custom-call(bf16[8192,128]{1,0:T(8,128)(2,1)} %fb.3, f32[4096,128]{1,0:T(8,128)} %get-tuple-element.56.own, bf16[4096,128]{1,0:T(8,128)(2,1)} %collective-permute-done.32.left, bf16[4096,128]{1,0:T(8,128)(2,1)} %collective-permute-done.34.right, ...), custom_call_target="tpu_custom_call" | custom-call | flops 402653184 | bytes 7340032 | tf_op jit(solution)/shard_map/merge/pallas_call | solution.py:167
  136.2 5.7 %collective-permute-start.35 = (f32[32,4096]{1,0:T(8,128)}, f32[32,4096]{1,0:T(8,128)S(1)}, u32[]{:S(2)}, u32[]{:S(2)}) collective-permute-start(f32[32,4096]{1,0:T(8,128)} %get-tuple-element.62), channel_id=1, source_target_pairs={{0,16},{16,0},{32,48},{48,32},{64,80},{80,64},{96,112},{112,96},{1... | collective-permute-start | bytes 1572872 | tf_op jit(solution)/shard_map/ppermute | solution.py:34
  141.9 5.7 %merge.2 = (f32[4096,128]{1,0:T(8,128)}, f32[32,4096]{1,0:T(8,128)}, f32[32,4096]{1,0:T(8,128)}) custom-call(bf16[8192,128]{1,0:T(8,128)(2,1)} %fb.3, f32[4096,128]{1,0:T(8,128)} %get-tuple-element.47.own, bf16[4096,128]{1,0:T(8,128)(2,1)} %collective-permute-done.19.left, bf16[4096,128]{1,0:T(8,128)(2,1)} %collective-permute-done.21.right, ...), custom_call_target="tpu_custom_call" | custom-call | flops 402653184 | bytes 7340032 | tf_op jit(solution)/shard_map/merge/pallas_call | solution.py:167
  148.5 2.5 collective-permute-start.38
  151.0 1.6 collective-permute-start.36
  155.5 6.7 %collective-permute-done.38 = bf16[32,4096]{1,0:T(8,128)(2,1)S(1)} collective-permute-done((bf16[32,4096]{1,0:T(8,128)(2,1)S(1)}, bf16[32,4096]{1,0:T(8,128)(2,1)S(1)}, u32[]{:S(2)}, u32[]{:S(2)}) %collective-permute-start.38) | collective-permute-done | bytes 262176 | tf_op jit(solution)/shard_map/ppermute | solution.py:34
  162.2 2.8 %collective-permute-done.37 = bf16[32,4096]{1,0:T(8,128)(2,1)S(1)} collective-permute-done((bf16[32,4096]{1,0:T(8,128)(2,1)S(1)}, bf16[32,4096]{1,0:T(8,128)(2,1)S(1)}, u32[]{:S(2)}, u32[]{:S(2)}) %collective-permute-start.37) | collective-permute-done | bytes 262176 | tf_op jit(solution)/shard_map/ppermute | solution.py:34
  165.1 2.4 collective-permute-start.39
  167.5 5.9 %collective-permute-done.25 = bf16[32,4096]{1,0:T(8,128)(2,1)S(1)} collective-permute-done((bf16[32,4096]{1,0:T(8,128)(2,1)S(1)}, bf16[32,4096]{1,0:T(8,128)(2,1)S(1)}, u32[]{:S(2)}, u32[]{:S(2)}) %collective-permute-start.25) | collective-permute-done | bytes 262176 | tf_op jit(solution)/shard_map/ppermute | solution.py:34
  173.4 3.2 %collective-permute-done.24 = bf16[32,4096]{1,0:T(8,128)(2,1)S(1)} collective-permute-done((bf16[32,4096]{1,0:T(8,128)(2,1)S(1)}, bf16[32,4096]{1,0:T(8,128)(2,1)S(1)}, u32[]{:S(2)}, u32[]{:S(2)}) %collective-permute-start.24) | collective-permute-done | bytes 262176 | tf_op jit(solution)/shard_map/ppermute | solution.py:34
  178.0 1.5 collective-permute-done.26
  180.8 4.7 %gram.2 = (f32[64,64]{1,0:T(8,128)}, f32[64,128]{1,0:T(8,128)}) custom-call(f32[64,4096]{1,0:T(8,128)} %pad_maximum_fusion.7.pt.pt_a, f32[4096,128]{1,0:T(8,128)} %get-tuple-element.54.merged.mg_a), custom_call_target="tpu_custom_call" | custom-call | flops 603979776 | bytes 3145728 | tf_op jit(solution)/shard_map/gram/pallas_call | solution.py:208
  186.5 8.2 %input_parts.3 = (f32[128,4096]{1,0:T(8,128)}, bf16[128,4096]{1,0:T(8,128)(2,1)}, bf16[64,4096]{1,0:T(8,128)(2,1)}, bf16[64,4096]{1,0:T(8,128)(2,1)}, bf16[128,4096]{1,0:T(8,128)(2,1)}) custom-call(bf16[8192,128]{1,0:T(8,128)(2,1)} %w0.3, bf16[8,6,512,128]{3,2,1,0:T(8,128)(2,1)} %bitcast.53, bf16[512,512]{1,0:T(8,128)(2,1)} %pad_maximum_fusion.12.cmat), custom_call_target="tpu_custom_call" | custom-call | flops 2147483648 | bytes 9437184 | tf_op jit(solution)/shard_map/input_parts/pallas_call | solution.py:126
  194.8 3.5 %collective-permute-start.12 = (bf16[64,4096]{1,0:T(8,128)(2,1)}, bf16[64,4096]{1,0:T(8,128)(2,1)}, u32[]{:S(2)}, u32[]{:S(2)}) collective-permute-start(bf16[64,4096]{1,0:T(8,128)(2,1)} %get-tuple-element.46), channel_id=1, source_target_pairs={{0,12},{1,13},{2,14},{3,15},{4,0},{5,1},{6,2},{7,3},{8,4},{9,5},{1... | collective-permute-start | bytes 1572872 | tf_op jit(solution)/shard_map/ppermute | solution.py:25
  198.3 4.7 %gram.3 = (f32[64,64]{1,0:T(8,128)}, f32[64,128]{1,0:T(8,128)}) custom-call(f32[64,4096]{1,0:T(8,128)} %pad_maximum_fusion.10.pt.pt_b, f32[4096,128]{1,0:T(8,128)} %get-tuple-element.63.merged.mg_b), custom_call_target="tpu_custom_call" | custom-call | flops 603979776 | bytes 3145728 | tf_op jit(solution)/shard_map/gram/pallas_call | solution.py:208
  205.3 2.7 collective-permute-start.43
  208.0 6.8 %inverse_factor.1.inv = f32[64,64]{1,0:T(8,128)} custom-call(f32[64,64]{1,0:T(8,128)} %get-tuple-element.55.gram_a, f32[64,64]{1,0:T(8,128)} %get-tuple-element.64.gram_b), custom_call_target="tpu_custom_call" | custom-call | flops 104857600 | bytes 65536 | tf_op jit(solution)/shard_map/inverse_factor/pallas_call | solution.py:238
  215.6 8.2 %input_parts.2 = (f32[128,4096]{1,0:T(8,128)}, bf16[128,4096]{1,0:T(8,128)(2,1)}, bf16[64,4096]{1,0:T(8,128)(2,1)}, bf16[64,4096]{1,0:T(8,128)(2,1)}, bf16[128,4096]{1,0:T(8,128)(2,1)}) custom-call(bf16[8192,128]{1,0:T(8,128)(2,1)} %w0.3, bf16[8,6,512,128]{3,2,1,0:T(8,128)(2,1)} %bitcast.54, bf16[512,512]{1,0:T(8,128)(2,1)} %pad_maximum_fusion.11.cmat), custom_call_target="tpu_custom_call" | custom-call | flops 2147483648 | bytes 9437184 | tf_op jit(solution)/shard_map/input_parts/pallas_call | solution.py:126
  229.8 2.6 collective-permute-start.13
  234.7 1.9 collective-permute-done.8
  237.8 1.7 collective-permute-start.9
  241.3 9.9 %final.1 = (f32[64,128]{1,0:T(8,128)}, bf16[8192,128]{1,0:T(8,128)(2,1)}, bf16[8192,128]{1,0:T(8,128)(2,1)}) custom-call(f32[64,64]{1,0:T(8,128)} %inverse_factor.1.inv, f32[64,128]{1,0:T(8,128)} %add_add_fusion.2.rsum, f32[64,4096]{1,0:T(8,128)} %pad_maximum_fusion.7.pt.pt_a, f32[64,4096]{1,0:T(8,128)} %pad_maximum_fusion.10.pt.pt_b, ...), custom_call_target="tpu_custom_call" | custom-call | flops 805306368 | bytes 12582912 | tf_op jit(solution)/shard_map/final/pallas_call | solution.py:280
  251.2 2.3 collective-permute-done.13
  253.5 5.4 %collective-permute-done.11 = bf16[128,4096]{1,0:T(8,128)(2,1)} collective-permute-done((bf16[128,4096]{1,0:T(8,128)(2,1)}, bf16[128,4096]{1,0:T(8,128)(2,1)}, u32[]{:S(2)}, u32[]{:S(2)}) %collective-permute-start.11) | collective-permute-done | bytes 1048608 | tf_op jit(solution)/shard_map/ppermute | solution.py:25
  258.9 1.7 add_convert_fusion
  261.0 4.1 %collective-permute-done.7 = bf16[128,4096]{1,0:T(8,128)(2,1)} collective-permute-done((bf16[128,4096]{1,0:T(8,128)(2,1)}, bf16[128,4096]{1,0:T(8,128)(2,1)}, u32[]{:S(2)}, u32[]{:S(2)}) %collective-permute-start.7) | collective-permute-done | bytes 1048608 | tf_op jit(solution)/shard_map/ppermute | solution.py:25
  265.1 2.0 add_convert_fusion.1
  (162 shorter events, 42.9 us)
Async XLA Ops:
  7.2 179.4 %all-gather.3.cloned.1.call-start = ((), (), s32[]{:S(2)}) async-start(), calls=%async_computation | async-start | bytes 7077888 | tf_op jit(solution)/shard_map/all_gather | solution.py:385
  10.0 42.5 %copy-start.12 = (bf16[128,4096]{1,0:T(8,128)(2,1)}, bf16[128,4096]{1,0:T(8,128)(2,1)S(1)}, u32[]{:S(2)}) copy-start(bf16[128,4096]{1,0:T(8,128)(2,1)S(1)} %get-tuple-element.71.a0) | copy-start | bytes 3145732
  10.0 51.0 %collective-permute-start.27 = (bf16[128,4096]{1,0:T(8,128)(2,1)}, bf16[128,4096]{1,0:T(8,128)(2,1)}, u32[]{:S(2)}, u32[]{:S(2)}) collective-permute-start(bf16[128,4096]{1,0:T(8,128)(2,1)} %get-tuple-element.70.a0), channel_id=1, source_target_pairs={{0,12},{1,13},{2,14},{3,15},{4,0},{5,1},{6,2},{7,3},{8,4},{9,5},{1... | collective-permute-start | bytes 3145736 | tf_op jit(solution)/shard_map/ppermute | solution.py:25
  14.6 45.3 %collective-permute-start.28 = (bf16[128,4096]{1,0:T(8,128)(2,1)}, bf16[128,4096]{1,0:T(8,128)(2,1)}, u32[]{:S(2)}, u32[]{:S(2)}) collective-permute-start(bf16[128,4096]{1,0:T(8,128)(2,1)} %get-tuple-element.70.a0), channel_id=1, source_target_pairs={{0,4},{1,5},{2,6},{3,7},{4,8},{5,9},{6,10},{7,11},{8,12},{9,13},{1... | collective-permute-start | bytes 3145736 | tf_op jit(solution)/shard_map/ppermute | solution.py:25
  16.1 26.1 %collective-permute-start = (bf16[1024,128]{1,0:T(8,128)(2,1)S(1)}, bf16[1024,128]{1,0:T(8,128)(2,1)S(1)}, u32[]{:S(2)}, u32[]{:S(2)}) collective-permute-start(bf16[1024,128]{1,0:T(8,128)(2,1)S(1)} %get-tuple-element.91), channel_id=1, source_target_pairs={{0,12},{1,13},{2,14},{3,15},{4,0},{5,1},{6,2},{7,3},{8,4},{9,5},{1... | collective-permute-start | bytes 786440 | tf_op jit(solution)/shard_map/ppermute | solution.py:25
  18.9 26.0 %collective-permute-start.4 = (bf16[1024,128]{1,0:T(8,128)(2,1)S(1)}, bf16[1024,128]{1,0:T(8,128)(2,1)S(1)}, u32[]{:S(2)}, u32[]{:S(2)}) collective-permute-start(bf16[1024,128]{1,0:T(8,128)(2,1)S(1)} %get-tuple-element.87), channel_id=1, source_target_pairs={{0,2},{1,3},{2,0},{3,1},{4,6},{5,7},{6,4},{7,5},{8,10},{9,11},{10,... | collective-permute-start | bytes 786440 | tf_op jit(solution)/shard_map/ppermute | solution.py:25
  21.9 25.1 %collective-permute-start.5 = (bf16[1024,128]{1,0:T(8,128)(2,1)S(1)}, bf16[1024,128]{1,0:T(8,128)(2,1)S(1)}, u32[]{:S(2)}, u32[]{:S(2)}) collective-permute-start(bf16[1024,128]{1,0:T(8,128)(2,1)S(1)} %get-tuple-element.86), channel_id=1, source_target_pairs={{0,1},{1,2},{2,3},{3,0},{4,5},{5,6},{6,7},{7,4},{8,9},{9,10},{10,1... | collective-permute-start | bytes 786440 | tf_op jit(solution)/shard_map/ppermute | solution.py:25
  42.2 23.5 %copy-start.15 = (bf16[1024,128]{1,0:T(8,128)(2,1)}, bf16[1024,128]{1,0:T(8,128)(2,1)S(1)}, u32[]{:S(2)}) copy-start(bf16[1024,128]{1,0:T(8,128)(2,1)S(1)} %collective-permute-done) | copy-start | bytes 786436
  42.2 6.8 %collective-permute-start.3 = (bf16[1024,128]{1,0:T(8,128)(2,1)S(1)}, bf16[1024,128]{1,0:T(8,128)(2,1)S(1)}, u32[]{:S(2)}, u32[]{:S(2)}) collective-permute-start(bf16[1024,128]{1,0:T(8,128)(2,1)S(1)} %get-tuple-element.88), channel_id=1, source_target_pairs={{0,3},{1,0},{2,1},{3,2},{4,7},{5,4},{6,5},{7,6},{8,11},{9,8},{10,9... | collective-permute-start | bytes 786440 | tf_op jit(solution)/shard_map/ppermute | solution.py:25
  44.9 7.5 %collective-permute-start.1 = (bf16[1024,128]{1,0:T(8,128)(2,1)S(1)}, bf16[1024,128]{1,0:T(8,128)(2,1)S(1)}, u32[]{:S(2)}, u32[]{:S(2)}) collective-permute-start(bf16[1024,128]{1,0:T(8,128)(2,1)S(1)} %get-tuple-element.90), channel_id=1, source_target_pairs={{0,8},{1,9},{2,10},{3,11},{4,12},{5,13},{6,14},{7,15},{8,0},{9,1},... | collective-permute-start | bytes 786440 | tf_op jit(solution)/shard_map/ppermute | solution.py:25
  47.0 12.8 %collective-permute-start.2 = (bf16[1024,128]{1,0:T(8,128)(2,1)S(1)}, bf16[1024,128]{1,0:T(8,128)(2,1)S(1)}, u32[]{:S(2)}, u32[]{:S(2)}) collective-permute-start(bf16[1024,128]{1,0:T(8,128)(2,1)S(1)} %get-tuple-element.89), channel_id=1, source_target_pairs={{0,4},{1,5},{2,6},{3,7},{4,8},{5,9},{6,10},{7,11},{8,12},{9,13},{1... | collective-permute-start | bytes 786440 | tf_op jit(solution)/shard_map/ppermute | solution.py:25
  49.0 24.4 %collective-permute-start.15 = (bf16[128,4096]{1,0:T(8,128)(2,1)S(1)}, bf16[128,4096]{1,0:T(8,128)(2,1)S(1)}, u32[]{:S(2)}, u32[]{:S(2)}) collective-permute-start(bf16[128,4096]{1,0:T(8,128)(2,1)S(1)} %get-tuple-element.71.a0), channel_id=1, source_target_pairs={{0,1},{1,2},{2,3},{3,0},{4,5},{5,6},{6,7},{7,4},{8,9},{9,10},{10,1... | collective-permute-start | bytes 3145736 | tf_op jit(solution)/shard_map/ppermute | solution.py:25
  52.4 21.9 %collective-permute-start.14 = (bf16[128,4096]{1,0:T(8,128)(2,1)S(1)}, bf16[128,4096]{1,0:T(8,128)(2,1)S(1)}, u32[]{:S(2)}, u32[]{:S(2)}) collective-permute-start(bf16[128,4096]{1,0:T(8,128)(2,1)S(1)} %get-tuple-element.71.a0), channel_id=1, source_target_pairs={{0,3},{1,0},{2,1},{3,2},{4,7},{5,4},{6,5},{7,6},{8,11},{9,8},{10,9... | collective-permute-start | bytes 3145736 | tf_op jit(solution)/shard_map/ppermute | solution.py:25
  60.9 17.0 %collective-permute-start.29 = (bf16[64,4096]{1,0:T(8,128)(2,1)S(1)}, bf16[64,4096]{1,0:T(8,128)(2,1)S(1)}, u32[]{:S(2)}, u32[]{:S(2)}) collective-permute-start(bf16[64,4096]{1,0:T(8,128)(2,1)S(1)} %slice.200), channel_id=1, source_target_pairs={{0,4},{1,5},{2,6},{3,7},{4,8},{5,9},{6,10},{7,11},{8,12},{9,13},{1... | collective-permute-start | bytes 1572872 | tf_op jit(solution)/shard_map/ppermute | solution.py:25
  62.1 16.6 %collective-permute-start.30 = (bf16[64,4096]{1,0:T(8,128)(2,1)S(1)}, bf16[64,4096]{1,0:T(8,128)(2,1)}, u32[]{:S(2)}, u32[]{:S(2)}) collective-permute-start(bf16[64,4096]{1,0:T(8,128)(2,1)S(1)} %slice.201), channel_id=1, source_target_pairs={{0,12},{1,13},{2,14},{3,15},{4,0},{5,1},{6,2},{7,3},{8,4},{9,5},{1... | collective-permute-start | bytes 1572872 | tf_op jit(solution)/shard_map/ppermute | solution.py:25
  74.3 18.5 %collective-permute-start.16 = (bf16[64,4096]{1,0:T(8,128)(2,1)}, bf16[64,4096]{1,0:T(8,128)(2,1)}, u32[]{:S(2)}, u32[]{:S(2)}) collective-permute-start(bf16[64,4096]{1,0:T(8,128)(2,1)} %slice.196), channel_id=1, source_target_pairs={{0,1},{1,2},{2,3},{3,0},{4,5},{5,6},{6,7},{7,4},{8,9},{9,10},{10,1... | collective-permute-start | bytes 1572872 | tf_op jit(solution)/shard_map/ppermute | solution.py:25
  75.2 17.6 %collective-permute-start.17 = (bf16[64,4096]{1,0:T(8,128)(2,1)}, bf16[64,4096]{1,0:T(8,128)(2,1)}, u32[]{:S(2)}, u32[]{:S(2)}) collective-permute-start(bf16[64,4096]{1,0:T(8,128)(2,1)} %slice.197), channel_id=1, source_target_pairs={{0,3},{1,0},{2,1},{3,2},{4,7},{5,4},{6,5},{7,6},{8,11},{9,8},{10,9... | collective-permute-start | bytes 1572872 | tf_op jit(solution)/shard_map/ppermute | solution.py:25
  87.5 20.1 %collective-permute-start.31 = (bf16[2048,128]{1,0:T(8,128)(2,1)}, bf16[2048,128]{1,0:T(8,128)(2,1)S(1)}, u32[]{:S(2)}, u32[]{:S(2)}) collective-permute-start(bf16[2048,128]{1,0:T(8,128)(2,1)} %get-tuple-element.58), channel_id=1, source_target_pairs={{0,1},{1,2},{2,3},{3,0},{4,5},{5,6},{6,7},{7,4},{8,9},{9,10},{10,1... | collective-permute-start | bytes 1572872 | tf_op jit(solution)/shard_map/ppermute | solution.py:25
  90.0 18.8 %collective-permute-start.33 = (bf16[2048,128]{1,0:T(8,128)(2,1)}, bf16[2048,128]{1,0:T(8,128)(2,1)}, u32[]{:S(2)}, u32[]{:S(2)}) collective-permute-start(bf16[2048,128]{1,0:T(8,128)(2,1)} %get-tuple-element.60), channel_id=1, source_target_pairs={{0,3},{1,0},{2,1},{3,2},{4,7},{5,4},{6,5},{7,6},{8,11},{9,8},{10,9... | collective-permute-start | bytes 1572872 | tf_op jit(solution)/shard_map/ppermute | solution.py:25
  102.9 12.0 %collective-permute-start.18 = (bf16[2048,128]{1,0:T(8,128)(2,1)}, bf16[2048,128]{1,0:T(8,128)(2,1)S(1)}, u32[]{:S(2)}, u32[]{:S(2)}) collective-permute-start(bf16[2048,128]{1,0:T(8,128)(2,1)} %get-tuple-element.49), channel_id=1, source_target_pairs={{0,4},{1,5},{2,6},{3,7},{4,8},{5,9},{6,10},{7,11},{8,12},{9,13},{1... | collective-permute-start | bytes 1572872 | tf_op jit(solution)/shard_map/ppermute | solution.py:25
  103.7 11.4 %collective-permute-start.20 = (bf16[2048,128]{1,0:T(8,128)(2,1)}, bf16[2048,128]{1,0:T(8,128)(2,1)S(1)}, u32[]{:S(2)}, u32[]{:S(2)}) collective-permute-start(bf16[2048,128]{1,0:T(8,128)(2,1)} %get-tuple-element.51), channel_id=1, source_target_pairs={{0,12},{1,13},{2,14},{3,15},{4,0},{5,1},{6,2},{7,3},{8,4},{9,5},{1... | collective-permute-start | bytes 1572872 | tf_op jit(solution)/shard_map/ppermute | solution.py:25
  108.8 21.6 %collective-permute-start.32 = (bf16[4096,128]{1,0:T(8,128)(2,1)}, bf16[4096,128]{1,0:T(8,128)(2,1)}, u32[]{:S(2)}, u32[]{:S(2)}) collective-permute-start(bf16[4096,128]{1,0:T(8,128)(2,1)} %pad_maximum_fusion.8), channel_id=1, source_target_pairs={{0,1},{1,2},{2,3},{3,0},{4,5},{5,6},{6,7},{7,4},{8,9},{9,10},{10,1... | collective-permute-start | bytes 3145736 | tf_op jit(solution)/shard_map/ppermute | solution.py:25
  110.2 20.3 %collective-permute-start.34 = (bf16[4096,128]{1,0:T(8,128)(2,1)S(1)}, bf16[4096,128]{1,0:T(8,128)(2,1)}, u32[]{:S(2)}, u32[]{:S(2)}) collective-permute-start(bf16[4096,128]{1,0:T(8,128)(2,1)S(1)} %pad_maximum_fusion.9), channel_id=1, source_target_pairs={{0,3},{1,0},{2,1},{3,2},{4,7},{5,4},{6,5},{7,6},{8,11},{9,8},{10,9... | collective-permute-start | bytes 3145736 | tf_op jit(solution)/shard_map/ppermute | solution.py:25
  115.0 26.9 %collective-permute-start.19 = (bf16[4096,128]{1,0:T(8,128)(2,1)S(1)}, bf16[4096,128]{1,0:T(8,128)(2,1)}, u32[]{:S(2)}, u32[]{:S(2)}) collective-permute-start(bf16[4096,128]{1,0:T(8,128)(2,1)S(1)} %pad_maximum_fusion.5), channel_id=1, source_target_pairs={{0,4},{1,5},{2,6},{3,7},{4,8},{5,9},{6,10},{7,11},{8,12},{9,13},{1... | collective-permute-start | bytes 3145736 | tf_op jit(solution)/shard_map/ppermute | solution.py:25
  116.3 25.6 %collective-permute-start.21 = (bf16[4096,128]{1,0:T(8,128)(2,1)}, bf16[4096,128]{1,0:T(8,128)(2,1)}, u32[]{:S(2)}, u32[]{:S(2)}) collective-permute-start(bf16[4096,128]{1,0:T(8,128)(2,1)} %pad_maximum_fusion.6), channel_id=1, source_target_pairs={{0,12},{1,13},{2,14},{3,15},{4,0},{5,1},{6,2},{7,3},{8,4},{9,5},{1... | collective-permute-start | bytes 3145736 | tf_op jit(solution)/shard_map/ppermute | solution.py:25
  136.2 12.2 %collective-permute-start.35 = (f32[32,4096]{1,0:T(8,128)}, f32[32,4096]{1,0:T(8,128)S(1)}, u32[]{:S(2)}, u32[]{:S(2)}) collective-permute-start(f32[32,4096]{1,0:T(8,128)} %get-tuple-element.62), channel_id=1, source_target_pairs={{0,16},{16,0},{32,48},{48,32},{64,80},{80,64},{96,112},{112,96},{1... | collective-permute-start | bytes 1572872 | tf_op jit(solution)/shard_map/ppermute | solution.py:34
  147.7 5.0 %collective-permute-start.22 = (f32[32,4096]{1,0:T(8,128)}, f32[32,4096]{1,0:T(8,128)S(1)}, u32[]{:S(2)}, u32[]{:S(2)}) collective-permute-start(f32[32,4096]{1,0:T(8,128)} %get-tuple-element.53), channel_id=1, source_target_pairs={{0,16},{16,0},{32,48},{48,32},{64,80},{80,64},{96,112},{112,96},{1... | collective-permute-start | bytes 1572872 | tf_op jit(solution)/shard_map/ppermute | solution.py:34
  148.5 13.7 %collective-permute-start.38 = (bf16[32,4096]{1,0:T(8,128)(2,1)S(1)}, bf16[32,4096]{1,0:T(8,128)(2,1)S(1)}, u32[]{:S(2)}, u32[]{:S(2)}) collective-permute-start(bf16[32,4096]{1,0:T(8,128)(2,1)S(1)} %add_convert_fusion.10), channel_id=1, source_target_pairs={{0,96},{16,112},{32,0},{48,16},{64,32},{80,48},{96,64},{112,80},{1... | collective-permute-start | bytes 786440 | tf_op jit(solution)/shard_map/ppermute | solution.py:34
  151.0 14.0 %collective-permute-start.37 = (bf16[32,4096]{1,0:T(8,128)(2,1)S(1)}, bf16[32,4096]{1,0:T(8,128)(2,1)S(1)}, u32[]{:S(2)}, u32[]{:S(2)}) collective-permute-start(bf16[32,4096]{1,0:T(8,128)(2,1)S(1)} %add_convert_fusion.10), channel_id=1, source_target_pairs={{0,32},{16,48},{32,64},{48,80},{64,96},{80,112},{96,0},{112,16},{1... | collective-permute-start | bytes 786440 | tf_op jit(solution)/shard_map/ppermute | solution.py:34
  151.0 14.0 %collective-permute-start.36 = (bf16[32,4096]{1,0:T(8,128)(2,1)S(1)}, bf16[32,4096]{1,0:T(8,128)(2,1)S(1)}, u32[]{:S(2)}, u32[]{:S(2)}) collective-permute-start(bf16[32,4096]{1,0:T(8,128)(2,1)S(1)} %add_convert_fusion.10), channel_id=1, source_target_pairs={{0,64},{16,80},{32,96},{48,112},{64,0},{80,16},{96,32},{112,48},{1... | collective-permute-start | bytes 786440 | tf_op jit(solution)/shard_map/ppermute | solution.py:34
  153.7 19.7 %collective-permute-start.25 = (bf16[32,4096]{1,0:T(8,128)(2,1)S(1)}, bf16[32,4096]{1,0:T(8,128)(2,1)S(1)}, u32[]{:S(2)}, u32[]{:S(2)}) collective-permute-start(bf16[32,4096]{1,0:T(8,128)(2,1)S(1)} %add_convert_fusion.11), channel_id=1, source_target_pairs={{0,96},{16,112},{32,0},{48,16},{64,32},{80,48},{96,64},{112,80},{1... | collective-permute-start | bytes 786440 | tf_op jit(solution)/shard_map/ppermute | solution.py:34
  154.9 21.8 %collective-permute-start.24 = (bf16[32,4096]{1,0:T(8,128)(2,1)S(1)}, bf16[32,4096]{1,0:T(8,128)(2,1)S(1)}, u32[]{:S(2)}, u32[]{:S(2)}) collective-permute-start(bf16[32,4096]{1,0:T(8,128)(2,1)S(1)} %add_convert_fusion.11), channel_id=1, source_target_pairs={{0,32},{16,48},{32,64},{48,80},{64,96},{80,112},{96,0},{112,16},{1... | collective-permute-start | bytes 786440 | tf_op jit(solution)/shard_map/ppermute | solution.py:34
  162.2 14.5 %collective-permute-start.23 = (bf16[32,4096]{1,0:T(8,128)(2,1)S(1)}, bf16[32,4096]{1,0:T(8,128)(2,1)S(1)}, u32[]{:S(2)}, u32[]{:S(2)}) collective-permute-start(bf16[32,4096]{1,0:T(8,128)(2,1)S(1)} %add_convert_fusion.11), channel_id=1, source_target_pairs={{0,64},{16,80},{32,96},{48,112},{64,0},{80,16},{96,32},{112,48},{1... | collective-permute-start | bytes 786440 | tf_op jit(solution)/shard_map/ppermute | solution.py:34
  165.1 12.9 %collective-permute-start.39 = (f32[32,4096]{1,0:T(8,128)S(1)}, f32[32,4096]{1,0:T(8,128)S(1)}, u32[]{:S(2)}, u32[]{:S(2)}) collective-permute-start(f32[32,4096]{1,0:T(8,128)S(1)} %add_add_fusion), channel_id=1, source_target_pairs={{0,16},{16,0},{32,48},{48,32},{64,80},{80,64},{96,112},{112,96},{1... | collective-permute-start | bytes 1572872 | tf_op jit(solution)/shard_map/ppermute | solution.py:34
  176.8 2.7 collective-permute-start.26
  194.8 20.7 %copy-start.5 = (bf16[128,4096]{1,0:T(8,128)(2,1)S(1)}, bf16[128,4096]{1,0:T(8,128)(2,1)}, u32[]{:S(2)}) copy-start(bf16[128,4096]{1,0:T(8,128)(2,1)} %get-tuple-element.45) | copy-start | bytes 3145732
  194.8 32.8 %collective-permute-start.12 = (bf16[64,4096]{1,0:T(8,128)(2,1)}, bf16[64,4096]{1,0:T(8,128)(2,1)}, u32[]{:S(2)}, u32[]{:S(2)}) collective-permute-start(bf16[64,4096]{1,0:T(8,128)(2,1)} %get-tuple-element.46), channel_id=1, source_target_pairs={{0,12},{1,13},{2,14},{3,15},{4,0},{5,1},{6,2},{7,3},{8,4},{9,5},{1... | collective-permute-start | bytes 1572872 | tf_op jit(solution)/shard_map/ppermute | solution.py:25
  203.8 1.5 collective-permute-start.40
  205.3 9.5 %collective-permute-start.42 = (f32[64,128]{1,0:T(8,128)S(1)}, f32[64,128]{1,0:T(8,128)S(1)}, u32[]{:S(2)}, u32[]{:S(2)}) collective-permute-start(f32[64,128]{1,0:T(8,128)S(1)} %add.124), channel_id=1, source_target_pairs={{0,32},{16,48},{32,64},{48,80},{64,96},{80,112},{96,0},{112,16},{1... | collective-permute-start | bytes 98312 | tf_op jit(solution)/shard_map/ppermute | solution.py:34
  205.3 9.5 %collective-permute-start.43 = (f32[64,128]{1,0:T(8,128)S(1)}, f32[64,128]{1,0:T(8,128)S(1)}, u32[]{:S(2)}, u32[]{:S(2)}) collective-permute-start(f32[64,128]{1,0:T(8,128)S(1)} %add.124), channel_id=1, source_target_pairs={{0,96},{16,112},{32,0},{48,16},{64,32},{80,48},{96,64},{112,80},{1... | collective-permute-start | bytes 98312 | tf_op jit(solution)/shard_map/ppermute | solution.py:34
  208.0 6.8 %collective-permute-start.41 = (f32[64,128]{1,0:T(8,128)S(1)}, f32[64,128]{1,0:T(8,128)S(1)}, u32[]{:S(2)}, u32[]{:S(2)}) collective-permute-start(f32[64,128]{1,0:T(8,128)S(1)} %add.124), channel_id=1, source_target_pairs={{0,64},{16,80},{32,96},{48,112},{64,0},{80,16},{96,32},{112,48},{1... | collective-permute-start | bytes 98312 | tf_op jit(solution)/shard_map/ppermute | solution.py:34
  215.5 17.0 %collective-permute-start.10 = (bf16[64,4096]{1,0:T(8,128)(2,1)}, bf16[64,4096]{1,0:T(8,128)(2,1)}, u32[]{:S(2)}, u32[]{:S(2)}) collective-permute-start(bf16[64,4096]{1,0:T(8,128)(2,1)} %get-tuple-element.44), channel_id=1, source_target_pairs={{0,4},{1,5},{2,6},{3,7},{4,8},{5,9},{6,10},{7,11},{8,12},{9,13},{1... | collective-permute-start | bytes 1572872 | tf_op jit(solution)/shard_map/ppermute | solution.py:25
  223.8 12.8 %collective-permute-start.8 = (bf16[64,4096]{1,0:T(8,128)(2,1)}, bf16[64,4096]{1,0:T(8,128)(2,1)S(1)}, u32[]{:S(2)}, u32[]{:S(2)}) collective-permute-start(bf16[64,4096]{1,0:T(8,128)(2,1)} %get-tuple-element.41), channel_id=1, source_target_pairs={{0,3},{1,0},{2,1},{3,2},{4,7},{5,4},{6,5},{7,6},{8,11},{9,8},{10,9... | collective-permute-start | bytes 1572872 | tf_op jit(solution)/shard_map/ppermute | solution.py:25
  226.9 13.2 %collective-permute-start.6 = (bf16[64,4096]{1,0:T(8,128)(2,1)S(1)}, bf16[64,4096]{1,0:T(8,128)(2,1)S(1)}, u32[]{:S(2)}, u32[]{:S(2)}) collective-permute-start(bf16[64,4096]{1,0:T(8,128)(2,1)S(1)} %copy-done.20), channel_id=1, source_target_pairs={{0,1},{1,2},{2,3},{3,0},{4,5},{5,6},{6,7},{7,4},{8,9},{9,10},{10,1... | collective-permute-start | bytes 1572872 | tf_op jit(solution)/shard_map/ppermute | solution.py:25
  229.8 23.7 %collective-permute-start.13 = (bf16[128,4096]{1,0:T(8,128)(2,1)}, bf16[128,4096]{1,0:T(8,128)(2,1)S(1)}, u32[]{:S(2)}, u32[]{:S(2)}) collective-permute-start(bf16[128,4096]{1,0:T(8,128)(2,1)} %pad_maximum_fusion.4), channel_id=1, source_target_pairs={{0,12},{1,13},{2,14},{3,15},{4,0},{5,1},{6,2},{7,3},{8,4},{9,5},{1... | collective-permute-start | bytes 3145736 | tf_op jit(solution)/shard_map/ppermute | solution.py:25
  234.7 24.1 %collective-permute-start.11 = (bf16[128,4096]{1,0:T(8,128)(2,1)}, bf16[128,4096]{1,0:T(8,128)(2,1)}, u32[]{:S(2)}, u32[]{:S(2)}) collective-permute-start(bf16[128,4096]{1,0:T(8,128)(2,1)} %pad_maximum_fusion.3), channel_id=1, source_target_pairs={{0,4},{1,5},{2,6},{3,7},{4,8},{5,9},{6,10},{7,11},{8,12},{9,13},{1... | collective-permute-start | bytes 3145736 | tf_op jit(solution)/shard_map/ppermute | solution.py:25
  237.8 23.2 %collective-permute-start.9 = (bf16[128,4096]{1,0:T(8,128)(2,1)}, bf16[128,4096]{1,0:T(8,128)(2,1)}, u32[]{:S(2)}, u32[]{:S(2)}) collective-permute-start(bf16[128,4096]{1,0:T(8,128)(2,1)} %pad_maximum_fusion.2), channel_id=1, source_target_pairs={{0,3},{1,0},{2,1},{3,2},{4,7},{5,4},{6,5},{7,6},{8,11},{9,8},{10,9... | collective-permute-start | bytes 3145736 | tf_op jit(solution)/shard_map/ppermute | solution.py:25
  241.3 23.8 %collective-permute-start.7 = (bf16[128,4096]{1,0:T(8,128)(2,1)}, bf16[128,4096]{1,0:T(8,128)(2,1)}, u32[]{:S(2)}, u32[]{:S(2)}) collective-permute-start(bf16[128,4096]{1,0:T(8,128)(2,1)} %pad_maximum_fusion.1), channel_id=1, source_target_pairs={{0,1},{1,2},{2,3},{3,0},{4,5},{5,6},{6,7},{7,4},{8,9},{9,10},{10,1... | collective-permute-start | bytes 3145736 | tf_op jit(solution)/shard_map/ppermute | solution.py:25
  (20 other events, 129.2 us)
Sparse Core Ops, SparseCore 0:
  88.7 46.3 all-gather.2
